TPU v7x, 32 devices: a whole 2x2x4 slice. The times are simulated.
32 devices in a mesh: lsec: 4 (over y, core), rsec: 8 (over z, x).
Axes of the slice: x: 2, y: 2, z: 4, core: 2. Of those that a mesh axis runs over, the one named last changes fastest.
Arguments:
- two_site: bfloat16 [2, 16, 128, 4096], P(None, 'lsec', None, 'rsec'), may hold values from -6 to 6
- left_env: bfloat16 [34, 16, 128, 128], P(None, 'lsec', 'rsec'), may hold values from -0.09375 to 0.09375
- right_env: bfloat16 [34, 32, 128, 128], P(None, 'rsec', 'lsec'), may hold values from -0.5 to 0.5
- left_size: int32 [16], P('lsec'), may hold values from 16 to 128, as said below
- right_size: int32 [32], P('rsec'), may hold values from 16 to 128, as said below
- channel_shift: int32 [34, 2], replicated, may hold values from -2 to 2, as said below
Outputs:
- applied: bfloat16 [2, 16, 128, 4096], P(None, 'lsec', None, 'rsec')
Inputs may be any that keep to these rules, and one draw needn't show every extreme that they name: `left_size`: each sector holds 16 to 128 states; some left sector and some right sector hold exactly 128. `right_size`: as for left_size. `channel_shift`: every offset from -2 to 2 is the left offset of some channel and the right offset of some channel.
All inputs are finite; a program needn't handle non-finite values.
Results may differ from a plain program's by a relative error of at most 0.0049.
Values may be sent and summed in bfloat16 or wider, within the bound.
A program may use at most 64 MiB of HBM per device.

v0:
```python
import jax
import jax.numpy as jnp
from jax import lax
from jax.sharding import PartitionSpec as P

KCH = 34
SHIFT = 2


def with_halo(value, sides, width):
    for axis, dim in sides:
        devices, length = (lax.axis_size(axis), value.shape[dim])
        up = [(i, (i + 1) % devices) for i in range(devices - 1)]
        down = [(j, i) for i, j in up]
        last = lax.slice_in_dim(value, length - width, length, axis=dim)
        first = lax.slice_in_dim(value, 0, width, axis=dim)
        before = lax.ppermute(last, axis, up)
        after = lax.ppermute(first, axis, down)
        value = jnp.concatenate([before, value, after], axis=dim)
    return value


def live_states(sizes, padded_extent):
    states = jnp.arange(padded_extent, dtype=jnp.int32)
    return (states[None, :] < sizes[:, None]).reshape(sizes.shape[0] * padded_extent)


def local(two_site, left_env, right_env, left_size, right_size, channel_shift):
    vectors, left_count, padded_extent, columns = two_site.shape
    right_count = columns // padded_extent
    row_live = live_states(left_size, padded_extent)
    col_live = live_states(right_size, padded_extent)
    weights = (row_live[:, None] & col_live[None, :]).astype(jnp.bfloat16)
    masked = two_site.reshape(vectors, left_count * padded_extent, columns) * weights[None]
    rim_width = SHIFT * padded_extent
    enlarged_operand = with_halo(masked, (("lsec", 1), ("rsec", 2)), rim_width)
    right_whole = lax.all_gather(right_env, "lsec", axis=2, tiled=True)

    def left_blocks(channel):
        own_piece = lax.dynamic_index_in_dim(left_env, channel, 0, keepdims=False)
        return lax.all_gather(own_piece, "rsec", axis=1, tiled=True)

    row_count = left_count * padded_extent

    def one_channel(channel, cumulative_sum):
        row_start = (SHIFT - channel_shift[channel, 0]) * padded_extent
        col_start = (SHIFT - channel_shift[channel, 1]) * padded_extent
        source = lax.dynamic_slice(
            enlarged_operand, (jnp.int32(0), row_start, col_start), (vectors, row_count, columns)
        )
        source = source.reshape(vectors, left_count, padded_extent, right_count, padded_extent)
        right_block = lax.dynamic_index_in_dim(right_whole, channel, 0, keepdims=False)
        right_reduced = jnp.einsum(
            "vlarb,rcb->vlarc", source, right_block, preferred_element_type=jnp.float32
        ).astype(jnp.bfloat16)
        left_sector_tensor = left_blocks(channel)
        return cumulative_sum + jnp.einsum(
            "jit,xjtum->xjium",
            left_sector_tensor,
            right_reduced,
            preferred_element_type=jnp.float32,
        )

    start_total = jnp.zeros(
        (vectors, left_count, padded_extent, right_count, padded_extent), jnp.float32
    )
    total = lax.fori_loop(0, KCH, one_channel, start_total)
    total = total.reshape(vectors, row_count, columns)
    row_float = row_live.astype(jnp.float32)
    col_float = col_live.astype(jnp.float32)
    result = (total * row_float[None, :, None] * col_float[None, None, :]).astype(jnp.bfloat16)
    return result.reshape(vectors, left_count, padded_extent, columns)


def solution(mesh):
    placed = (
        P(None, "lsec", None, "rsec"),
        P(None, "lsec", "rsec", None),
        P(None, "rsec", "lsec", None),
        P("lsec"),
        P("rsec"),
        P(),
    )
    return jax.shard_map(
        local, mesh=mesh, in_specs=placed, out_specs=P(None, "lsec", None, "rsec"), check_vma=False
    )
```

profile of v0, /device:TPU:0, one launch (start us, length us, event | category | flops | bytes accessed | tf_op | source)
XLA Modules:
  0.0 1392.3 jit_solution(2318776571986698694)
XLA Ops:
  25.5 39.7 %collective-permute-done.2 = bf16[2,1024,256]{2,1,0:T(8,128)(2,1)} collective-permute-done((bf16[2,1024,256]{2,1,0:T(8,128)(2,1)}, bf16[2,1024,256]{2,1,0:T(8,128)(2,1)}, u32[]{:S(2)}, u32[]{:S(2)}) %collective-permute-start.2) | collective-permute-done | bytes 1048608 | tf_op jit(solution)/shard_map/ppermute | solution.py:17
  68.7 1313.5 %while.14 = (s32[]{:T(128)}, f32[2,4,128,4,128]{2,4,3,0,1:T(8,128)}, bf16[34,4,128,128]{3,2,1,0:T(8,128)(2,1)}, s32[34,2]{0,1:T(2,128)S(1)}, bf16[2,1024,1024]{2...) while((s32[]{:T(128)}, ...), condition=%wide.region_1.2_spmd.clone, body=%wide.region_0.1_spmd.clone.sunk | while | flops 270008320 | bytes 9880331 | solution.py:67
  73.0 33.4 %all-gather.3 = bf16[1,4,128,128]{3,2,1,0:T(8,128)(2,1)S(1)} all-gather(bf16[1,4,16,128]{3,2,1,0:T(8,128)(2,1)S(1)} %constant_dynamic-slice_fusion.9), channel_id=2, replica_groups=mesh['lsec'=4,'rsec'=8] {'rsec'}, dimensions={2}, use_global_device_ids=true | all-gather | bytes 147456 | tf_op jit(solution)/shard_map/while/body/eval_jaxpr/all_gather | solution.py:41
  113.7 30.5 %all-gather.3 = bf16[1,4,128,128]{3,2,1,0:T(8,128)(2,1)S(1)} all-gather(bf16[1,4,16,128]{3,2,1,0:T(8,128)(2,1)S(1)} %constant_dynamic-slice_fusion.9), channel_id=2, replica_groups=mesh['lsec'=4,'rsec'=8] {'rsec'}, dimensions={2}, use_global_device_ids=true | all-gather | bytes 147456 | tf_op jit(solution)/shard_map/while/body/eval_jaxpr/all_gather | solution.py:41
  152.2 30.5 %all-gather.3 = bf16[1,4,128,128]{3,2,1,0:T(8,128)(2,1)S(1)} all-gather(bf16[1,4,16,128]{3,2,1,0:T(8,128)(2,1)S(1)} %constant_dynamic-slice_fusion.9), channel_id=2, replica_groups=mesh['lsec'=4,'rsec'=8] {'rsec'}, dimensions={2}, use_global_device_ids=true | all-gather | bytes 147456 | tf_op jit(solution)/shard_map/while/body/eval_jaxpr/all_gather | solution.py:41
  190.8 30.6 %all-gather.3 = bf16[1,4,128,128]{3,2,1,0:T(8,128)(2,1)S(1)} all-gather(bf16[1,4,16,128]{3,2,1,0:T(8,128)(2,1)S(1)} %constant_dynamic-slice_fusion.9), channel_id=2, replica_groups=mesh['lsec'=4,'rsec'=8] {'rsec'}, dimensions={2}, use_global_device_ids=true | all-gather | bytes 147456 | tf_op jit(solution)/shard_map/while/body/eval_jaxpr/all_gather | solution.py:41
  229.4 30.6 %all-gather.3 = bf16[1,4,128,128]{3,2,1,0:T(8,128)(2,1)S(1)} all-gather(bf16[1,4,16,128]{3,2,1,0:T(8,128)(2,1)S(1)} %constant_dynamic-slice_fusion.9), channel_id=2, replica_groups=mesh['lsec'=4,'rsec'=8] {'rsec'}, dimensions={2}, use_global_device_ids=true | all-gather | bytes 147456 | tf_op jit(solution)/shard_map/while/body/eval_jaxpr/all_gather | solution.py:41
  268.0 30.6 %all-gather.3 = bf16[1,4,128,128]{3,2,1,0:T(8,128)(2,1)S(1)} all-gather(bf16[1,4,16,128]{3,2,1,0:T(8,128)(2,1)S(1)} %constant_dynamic-slice_fusion.9), channel_id=2, replica_groups=mesh['lsec'=4,'rsec'=8] {'rsec'}, dimensions={2}, use_global_device_ids=true | all-gather | bytes 147456 | tf_op jit(solution)/shard_map/while/body/eval_jaxpr/all_gather | solution.py:41
  306.6 30.6 %all-gather.3 = bf16[1,4,128,128]{3,2,1,0:T(8,128)(2,1)S(1)} all-gather(bf16[1,4,16,128]{3,2,1,0:T(8,128)(2,1)S(1)} %constant_dynamic-slice_fusion.9), channel_id=2, replica_groups=mesh['lsec'=4,'rsec'=8] {'rsec'}, dimensions={2}, use_global_device_ids=true | all-gather | bytes 147456 | tf_op jit(solution)/shard_map/while/body/eval_jaxpr/all_gather | solution.py:41
  345.3 30.5 %all-gather.3 = bf16[1,4,128,128]{3,2,1,0:T(8,128)(2,1)S(1)} all-gather(bf16[1,4,16,128]{3,2,1,0:T(8,128)(2,1)S(1)} %constant_dynamic-slice_fusion.9), channel_id=2, replica_groups=mesh['lsec'=4,'rsec'=8] {'rsec'}, dimensions={2}, use_global_device_ids=true | all-gather | bytes 147456 | tf_op jit(solution)/shard_map/while/body/eval_jaxpr/all_gather | solution.py:41
  383.8 30.5 %all-gather.3 = bf16[1,4,128,128]{3,2,1,0:T(8,128)(2,1)S(1)} all-gather(bf16[1,4,16,128]{3,2,1,0:T(8,128)(2,1)S(1)} %constant_dynamic-slice_fusion.9), channel_id=2, replica_groups=mesh['lsec'=4,'rsec'=8] {'rsec'}, dimensions={2}, use_global_device_ids=true | all-gather | bytes 147456 | tf_op jit(solution)/shard_map/while/body/eval_jaxpr/all_gather | solution.py:41
  422.4 30.5 %all-gather.3 = bf16[1,4,128,128]{3,2,1,0:T(8,128)(2,1)S(1)} all-gather(bf16[1,4,16,128]{3,2,1,0:T(8,128)(2,1)S(1)} %constant_dynamic-slice_fusion.9), channel_id=2, replica_groups=mesh['lsec'=4,'rsec'=8] {'rsec'}, dimensions={2}, use_global_device_ids=true | all-gather | bytes 147456 | tf_op jit(solution)/shard_map/while/body/eval_jaxpr/all_gather | solution.py:41
  460.9 30.5 %all-gather.3 = bf16[1,4,128,128]{3,2,1,0:T(8,128)(2,1)S(1)} all-gather(bf16[1,4,16,128]{3,2,1,0:T(8,128)(2,1)S(1)} %constant_dynamic-slice_fusion.9), channel_id=2, replica_groups=mesh['lsec'=4,'rsec'=8] {'rsec'}, dimensions={2}, use_global_device_ids=true | all-gather | bytes 147456 | tf_op jit(solution)/shard_map/while/body/eval_jaxpr/all_gather | solution.py:41
  499.5 30.5 %all-gather.3 = bf16[1,4,128,128]{3,2,1,0:T(8,128)(2,1)S(1)} all-gather(bf16[1,4,16,128]{3,2,1,0:T(8,128)(2,1)S(1)} %constant_dynamic-slice_fusion.9), channel_id=2, replica_groups=mesh['lsec'=4,'rsec'=8] {'rsec'}, dimensions={2}, use_global_device_ids=true | all-gather | bytes 147456 | tf_op jit(solution)/shard_map/while/body/eval_jaxpr/all_gather | solution.py:41
  538.0 30.5 %all-gather.3 = bf16[1,4,128,128]{3,2,1,0:T(8,128)(2,1)S(1)} all-gather(bf16[1,4,16,128]{3,2,1,0:T(8,128)(2,1)S(1)} %constant_dynamic-slice_fusion.9), channel_id=2, replica_groups=mesh['lsec'=4,'rsec'=8] {'rsec'}, dimensions={2}, use_global_device_ids=true | all-gather | bytes 147456 | tf_op jit(solution)/shard_map/while/body/eval_jaxpr/all_gather | solution.py:41
  576.6 30.5 %all-gather.3 = bf16[1,4,128,128]{3,2,1,0:T(8,128)(2,1)S(1)} all-gather(bf16[1,4,16,128]{3,2,1,0:T(8,128)(2,1)S(1)} %constant_dynamic-slice_fusion.9), channel_id=2, replica_groups=mesh['lsec'=4,'rsec'=8] {'rsec'}, dimensions={2}, use_global_device_ids=true | all-gather | bytes 147456 | tf_op jit(solution)/shard_map/while/body/eval_jaxpr/all_gather | solution.py:41
  615.1 30.5 %all-gather.3 = bf16[1,4,128,128]{3,2,1,0:T(8,128)(2,1)S(1)} all-gather(bf16[1,4,16,128]{3,2,1,0:T(8,128)(2,1)S(1)} %constant_dynamic-slice_fusion.9), channel_id=2, replica_groups=mesh['lsec'=4,'rsec'=8] {'rsec'}, dimensions={2}, use_global_device_ids=true | all-gather | bytes 147456 | tf_op jit(solution)/shard_map/while/body/eval_jaxpr/all_gather | solution.py:41
  653.6 30.5 %all-gather.3 = bf16[1,4,128,128]{3,2,1,0:T(8,128)(2,1)S(1)} all-gather(bf16[1,4,16,128]{3,2,1,0:T(8,128)(2,1)S(1)} %constant_dynamic-slice_fusion.9), channel_id=2, replica_groups=mesh['lsec'=4,'rsec'=8] {'rsec'}, dimensions={2}, use_global_device_ids=true | all-gather | bytes 147456 | tf_op jit(solution)/shard_map/while/body/eval_jaxpr/all_gather | solution.py:41
  692.2 30.5 %all-gather.3 = bf16[1,4,128,128]{3,2,1,0:T(8,128)(2,1)S(1)} all-gather(bf16[1,4,16,128]{3,2,1,0:T(8,128)(2,1)S(1)} %constant_dynamic-slice_fusion.9), channel_id=2, replica_groups=mesh['lsec'=4,'rsec'=8] {'rsec'}, dimensions={2}, use_global_device_ids=true | all-gather | bytes 147456 | tf_op jit(solution)/shard_map/while/body/eval_jaxpr/all_gather | solution.py:41
  730.7 30.5 %all-gather.3 = bf16[1,4,128,128]{3,2,1,0:T(8,128)(2,1)S(1)} all-gather(bf16[1,4,16,128]{3,2,1,0:T(8,128)(2,1)S(1)} %constant_dynamic-slice_fusion.9), channel_id=2, replica_groups=mesh['lsec'=4,'rsec'=8] {'rsec'}, dimensions={2}, use_global_device_ids=true | all-gather | bytes 147456 | tf_op jit(solution)/shard_map/while/body/eval_jaxpr/all_gather | solution.py:41
  769.3 30.6 %all-gather.3 = bf16[1,4,128,128]{3,2,1,0:T(8,128)(2,1)S(1)} all-gather(bf16[1,4,16,128]{3,2,1,0:T(8,128)(2,1)S(1)} %constant_dynamic-slice_fusion.9), channel_id=2, replica_groups=mesh['lsec'=4,'rsec'=8] {'rsec'}, dimensions={2}, use_global_device_ids=true | all-gather | bytes 147456 | tf_op jit(solution)/shard_map/while/body/eval_jaxpr/all_gather | solution.py:41
  807.9 30.5 %all-gather.3 = bf16[1,4,128,128]{3,2,1,0:T(8,128)(2,1)S(1)} all-gather(bf16[1,4,16,128]{3,2,1,0:T(8,128)(2,1)S(1)} %constant_dynamic-slice_fusion.9), channel_id=2, replica_groups=mesh['lsec'=4,'rsec'=8] {'rsec'}, dimensions={2}, use_global_device_ids=true | all-gather | bytes 147456 | tf_op jit(solution)/shard_map/while/body/eval_jaxpr/all_gather | solution.py:41
  846.5 30.6 %all-gather.3 = bf16[1,4,128,128]{3,2,1,0:T(8,128)(2,1)S(1)} all-gather(bf16[1,4,16,128]{3,2,1,0:T(8,128)(2,1)S(1)} %constant_dynamic-slice_fusion.9), channel_id=2, replica_groups=mesh['lsec'=4,'rsec'=8] {'rsec'}, dimensions={2}, use_global_device_ids=true | all-gather | bytes 147456 | tf_op jit(solution)/shard_map/while/body/eval_jaxpr/all_gather | solution.py:41
  885.1 30.6 %all-gather.3 = bf16[1,4,128,128]{3,2,1,0:T(8,128)(2,1)S(1)} all-gather(bf16[1,4,16,128]{3,2,1,0:T(8,128)(2,1)S(1)} %constant_dynamic-slice_fusion.9), channel_id=2, replica_groups=mesh['lsec'=4,'rsec'=8] {'rsec'}, dimensions={2}, use_global_device_ids=true | all-gather | bytes 147456 | tf_op jit(solution)/shard_map/while/body/eval_jaxpr/all_gather | solution.py:41
  923.6 30.6 %all-gather.3 = bf16[1,4,128,128]{3,2,1,0:T(8,128)(2,1)S(1)} all-gather(bf16[1,4,16,128]{3,2,1,0:T(8,128)(2,1)S(1)} %constant_dynamic-slice_fusion.9), channel_id=2, replica_groups=mesh['lsec'=4,'rsec'=8] {'rsec'}, dimensions={2}, use_global_device_ids=true | all-gather | bytes 147456 | tf_op jit(solution)/shard_map/while/body/eval_jaxpr/all_gather | solution.py:41
  962.3 30.5 %all-gather.3 = bf16[1,4,128,128]{3,2,1,0:T(8,128)(2,1)S(1)} all-gather(bf16[1,4,16,128]{3,2,1,0:T(8,128)(2,1)S(1)} %constant_dynamic-slice_fusion.9), channel_id=2, replica_groups=mesh['lsec'=4,'rsec'=8] {'rsec'}, dimensions={2}, use_global_device_ids=true | all-gather | bytes 147456 | tf_op jit(solution)/shard_map/while/body/eval_jaxpr/all_gather | solution.py:41
  1000.8 30.5 %all-gather.3 = bf16[1,4,128,128]{3,2,1,0:T(8,128)(2,1)S(1)} all-gather(bf16[1,4,16,128]{3,2,1,0:T(8,128)(2,1)S(1)} %constant_dynamic-slice_fusion.9), channel_id=2, replica_groups=mesh['lsec'=4,'rsec'=8] {'rsec'}, dimensions={2}, use_global_device_ids=true | all-gather | bytes 147456 | tf_op jit(solution)/shard_map/while/body/eval_jaxpr/all_gather | solution.py:41
  1039.4 30.5 %all-gather.3 = bf16[1,4,128,128]{3,2,1,0:T(8,128)(2,1)S(1)} all-gather(bf16[1,4,16,128]{3,2,1,0:T(8,128)(2,1)S(1)} %constant_dynamic-slice_fusion.9), channel_id=2, replica_groups=mesh['lsec'=4,'rsec'=8] {'rsec'}, dimensions={2}, use_global_device_ids=true | all-gather | bytes 147456 | tf_op jit(solution)/shard_map/while/body/eval_jaxpr/all_gather | solution.py:41
  1077.9 30.6 %all-gather.3 = bf16[1,4,128,128]{3,2,1,0:T(8,128)(2,1)S(1)} all-gather(bf16[1,4,16,128]{3,2,1,0:T(8,128)(2,1)S(1)} %constant_dynamic-slice_fusion.9), channel_id=2, replica_groups=mesh['lsec'=4,'rsec'=8] {'rsec'}, dimensions={2}, use_global_device_ids=true | all-gather | bytes 147456 | tf_op jit(solution)/shard_map/while/body/eval_jaxpr/all_gather | solution.py:41
  1116.6 30.6 %all-gather.3 = bf16[1,4,128,128]{3,2,1,0:T(8,128)(2,1)S(1)} all-gather(bf16[1,4,16,128]{3,2,1,0:T(8,128)(2,1)S(1)} %constant_dynamic-slice_fusion.9), channel_id=2, replica_groups=mesh['lsec'=4,'rsec'=8] {'rsec'}, dimensions={2}, use_global_device_ids=true | all-gather | bytes 147456 | tf_op jit(solution)/shard_map/while/body/eval_jaxpr/all_gather | solution.py:41
  1155.2 30.5 %all-gather.3 = bf16[1,4,128,128]{3,2,1,0:T(8,128)(2,1)S(1)} all-gather(bf16[1,4,16,128]{3,2,1,0:T(8,128)(2,1)S(1)} %constant_dynamic-slice_fusion.9), channel_id=2, replica_groups=mesh['lsec'=4,'rsec'=8] {'rsec'}, dimensions={2}, use_global_device_ids=true | all-gather | bytes 147456 | tf_op jit(solution)/shard_map/while/body/eval_jaxpr/all_gather | solution.py:41
  1193.8 30.5 %all-gather.3 = bf16[1,4,128,128]{3,2,1,0:T(8,128)(2,1)S(1)} all-gather(bf16[1,4,16,128]{3,2,1,0:T(8,128)(2,1)S(1)} %constant_dynamic-slice_fusion.9), channel_id=2, replica_groups=mesh['lsec'=4,'rsec'=8] {'rsec'}, dimensions={2}, use_global_device_ids=true | all-gather | bytes 147456 | tf_op jit(solution)/shard_map/while/body/eval_jaxpr/all_gather | solution.py:41
  (197 shorter events, 375.5 us)
Async XLA Ops:
  6.5 62.2 %all-gather.6.cloned.1.call-start = ((), (), s32[]{:S(2)}) async-start(), calls=%async_computation | async-start | bytes 5570560 | tf_op jit(solution)/shard_map/all_gather | solution.py:37
  10.3 3.9 collective-permute-start
  12.7 5.9 collective-permute-start.1
  19.8 45.4 %collective-permute-start.2 = (bf16[2,1024,256]{2,1,0:T(8,128)(2,1)}, bf16[2,1024,256]{2,1,0:T(8,128)(2,1)}, u32[]{:S(2)}, u32[]{:S(2)}) collective-permute-start(bf16[2,1024,256]{2,1,0:T(8,128)(2,1)} %get-tuple-element.150), channel_id=1, source_target_pairs={{0,1},{1,2},{2,3},{3,4},{4,5},{5,6},{6,7},{8,9},{9,10},{10,11},{11... | collective-permute-start | bytes 3145736 | tf_op jit(solution)/shard_map/ppermute | solution.py:17
  24.2 41.0 %collective-permute-start.3 = (bf16[2,1024,256]{2,1,0:T(8,128)(2,1)S(1)}, bf16[2,1024,256]{2,1,0:T(8,128)(2,1)}, u32[]{:S(2)}, u32[]{:S(2)}) collective-permute-start(bf16[2,1024,256]{2,1,0:T(8,128)(2,1)S(1)} %get-tuple-element.151), channel_id=1, source_target_pairs={{1,0},{2,1},{3,2},{4,3},{5,4},{6,5},{7,6},{9,8},{10,9},{11,10},{12... | collective-permute-start | bytes 3145736 | tf_op jit(solution)/shard_map/ppermute | solution.py:18
  25.5 43.2 %copy-start = (s32[34,2]{0,1:T(2,128)S(1)}, s32[34,2]{0,1:T(2,128)}, u32[]{:S(2)}) copy-start(s32[34,2]{0,1:T(2,128)} %param.13) | copy-start | bytes 820
Sparse Core Ops, SparseCore 0:
  8.9 42.4 all-gather.5
where the time goes:
time: 1400 us; the launch traced here: 1390 us
  blocking collectives  1040 us (74%)
  matrix products  128 us (9%)
  local copies, waits for them, and re-layouts  103 us (7%)
  waiting for transfers between devices  45 us (3%)
  loops' own time  44.5 us (3%)
    all_gather x34, blocking collectives, left_blocks(): return lax.all_gather(own_piece, 'rsec', axis=1, tiled=True)  1040 us
    dot_general x34, matrix products, one_channel(): jnp.einsum('jit,xjtum->xjium', left_sector_tensor, right_reduced, preferr...  128 us
    dynamic_slice x34, local copies, waits for them, and re-layouts, one_channel(): lax.dynamic_slice(enlarged_operand, (jnp.int32(0), row_start, col_start),...  44.9 us
    another operation x1, loops' own time, local(): total = lax.fori_loop(0, KCH, one_channel, start_total)  44.5 us
    ppermute x2, waiting for transfers between devices, with_halo(): before = lax.ppermute(last, axis, up)  39.9 us
  transfers between devices with their start and end apart: 5, of which 3 were waited for; matrix products, arithmetic and copies ran while one was open for 1% of the time, Pallas kernels for 0%

commit v1 on v0

v1 whole, which is shorter than its diff:
```python
import functools

import jax
import jax.numpy as jnp
from jax import lax
from jax.experimental import pallas as pl
from jax.experimental.pallas import tpu as pltpu
from jax.sharding import PartitionSpec as P

SHIFT = 2
GROUP = 2
AHEAD = 3
MESH = pl.DeviceIdType.MESH


def kernel(
    nl, nr, lsize, rsize, shift, x_hbm, l_hbm, r_hbm, out,
    xbuf, lbuf, rbuf, pbuf, acc,
    x_sem, own_sem, rh_send, rh_recv, lh_send, lh_recv,
    l1_send, l1_recv, l2_send, l2_recv, r1_send, r1_recv, r2_send, r2_recv,
):
    vectors, lc, sb, columns = x_hbm.shape
    rc = columns // sb
    channels = l_hbm.shape[0]
    eb = l_hbm.shape[1] // lc
    cb = r_hbm.shape[1] // rc
    chunks = channels // GROUP
    nz, ny = nr // 2, nl // 2
    lam = lax.axis_index("lsec")
    rho = lax.axis_index("rsec")
    mz, mx = rho // 2, rho % 2
    my, mc = lam // 2, lam % 2
    xpeer = mz * 2 + (1 - mx)
    cpeer = my * 2 + (1 - mc)
    S = SHIFT
    own_r, own_l = pl.ds(S, rc), pl.ds(S, lc)

    def zslot(j):
        return ((mz + (nz - j)) % nz) * 2 + mx

    def yslot(j):
        return ((my + (ny - j)) % ny) * 2 + mc

    def zto(j):
        return ((mz + j) % nz) * 2 + mx

    def yto(j):
        return ((my + j) % ny) * 2 + mc

    def remote(src, dst, send, recv, to):
        return pltpu.make_async_remote_copy(
            src_ref=src, dst_ref=dst, send_sem=send, recv_sem=recv,
            device_id=to, device_id_type=MESH,
        )

    x_copies = [
        pltpu.make_async_copy(
            x_hbm.at[:, :, :, pl.ds(r * sb, sb)], xbuf.at[S + r, :, own_l], x_sem.at[r]
        )
        for r in range(rc)
    ]
    for copy in x_copies:
        copy.start()
    own_l_copy = pltpu.make_async_copy(l_hbm, lbuf.at[rho], own_sem.at[0])
    own_r_copy = pltpu.make_async_copy(r_hbm, rbuf.at[lam], own_sem.at[1])
    own_l_copy.start()
    own_r_copy.start()

    has_up_r, has_dn_r = rho < nr - 1, rho > 0
    has_up_l, has_dn_l = lam < nl - 1, lam > 0
    far_r = jnp.where(mx == 1, rho + 1, rho + nr - 1) % nr
    far_l = jnp.where(mc == 1, lam + 1, lam + nl - 1) % nl

    barrier = pltpu.get_barrier_semaphore()
    near = [(lam, zto(j)) for j in range(1, nz)] + [(lam, xpeer)]
    near += [(yto(j), rho) for j in range(1, ny)] + [(cpeer, rho)]
    near += [(lam, far_r), (far_l, rho)]
    for to in near:
        pl.semaphore_signal(barrier, inc=1, device_id=to, device_id_type=MESH)

    def zero_r(at):
        xbuf[pl.ds(at, S)] = jnp.zeros((S,) + xbuf.shape[1:], xbuf.dtype)

    def zero_l(at):
        shape = (rc + 2 * S, vectors, S, sb, sb)
        xbuf[:, :, pl.ds(at, S)] = jnp.zeros(shape, xbuf.dtype)

    pl.when(rho == 0)(lambda: zero_r(0))
    pl.when(rho == nr - 1)(lambda: zero_r(S + rc))
    pl.when(lam == 0)(lambda: zero_l(0))
    pl.when(lam == nl - 1)(lambda: zero_l(S + lc))

    rows = lax.broadcasted_iota(jnp.int32, (sb, sb), 0)
    cols = lax.broadcasted_iota(jnp.int32, (sb, sb), 1)
    for r in range(rc):
        x_copies[r].wait()
        for l in range(lc):
            live = ((rows < lsize[l]) & (cols < rsize[r])).astype(jnp.float32)
            for v in range(vectors):
                block = xbuf[S + r, v, S + l].astype(jnp.float32)
                xbuf[S + r, v, S + l] = (block * live).astype(xbuf.dtype)

    pl.semaphore_wait(barrier, len(near))

    r_up = remote(
        xbuf.at[pl.ds(rc, S), :, own_l], xbuf.at[pl.ds(0, S), :, own_l],
        rh_send.at[0], rh_recv.at[0], (lam, rho + 1),
    )
    r_dn = remote(
        xbuf.at[pl.ds(S, S), :, own_l], xbuf.at[pl.ds(S + rc, S), :, own_l],
        rh_send.at[1], rh_recv.at[1], (lam, rho - 1),
    )

    def l_rim(part, at, count):
        up = remote(
            xbuf.at[pl.ds(at, count), :, pl.ds(lc, S)], xbuf.at[pl.ds(at, count), :, pl.ds(0, S)],
            lh_send.at[part, 0], lh_recv.at[part, 0], (lam + 1, rho),
        )
        dn = remote(
            xbuf.at[pl.ds(at, count), :, pl.ds(S, S)], xbuf.at[pl.ds(at, count), :, pl.ds(S + lc, S)],
            lh_send.at[part, 1], lh_recv.at[part, 1], (lam - 1, rho),
        )
        return up, dn

    l_mid = l_rim(0, S, rc)
    l_low = l_rim(1, 0, S)
    l_high = l_rim(2, S + rc, S)
    pl.when(has_up_r)(r_up.start)
    pl.when(has_dn_r)(r_dn.start)
    pl.when(has_up_l)(l_mid[0].start)
    pl.when(has_dn_l)(l_mid[1].start)

    def first_hop(c):
        part = pl.ds(c * GROUP, GROUP)
        copies = []
        for j in range(1, nz):
            copies.append(remote(
                l_hbm.at[part], lbuf.at[rho, part],
                l1_send.at[c, j - 1], l1_recv.at[c, j - 1], (lam, zto(j)),
            ))
        for j in range(1, ny):
            copies.append(remote(
                r_hbm.at[part], rbuf.at[lam, part],
                r1_send.at[c, j - 1], r1_recv.at[c, j - 1], (yto(j), rho),
            ))
        copies.append(remote(
            l_hbm.at[part], lbuf.at[rho, part],
            l2_send.at[c, 0], l2_recv.at[c, 0], (lam, xpeer),
        ))
        copies.append(remote(
            r_hbm.at[part], rbuf.at[lam, part],
            r2_send.at[c, 0], r2_recv.at[c, 0], (cpeer, rho),
        ))
        return copies

    def first_in(c):
        part = pl.ds(c * GROUP, GROUP)
        copies = []
        for j in range(1, nz):
            copies.append(remote(
                l_hbm.at[part], lbuf.at[zslot(j), part],
                l1_send.at[c, j - 1], l1_recv.at[c, j - 1], (lam, zto(j)),
            ))
        for j in range(1, ny):
            copies.append(remote(
                r_hbm.at[part], rbuf.at[yslot(j), part],
                r1_send.at[c, j - 1], r1_recv.at[c, j - 1], (yto(j), rho),
            ))
        return copies

    def second_hop(c):
        part = pl.ds(c * GROUP, GROUP)
        copies = []
        for j in range(1, nz):
            at = lbuf.at[zslot(j), part]
            copies.append(remote(at, at, l2_send.at[c, j], l2_recv.at[c, j], (lam, xpeer)))
        for j in range(1, ny):
            at = rbuf.at[yslot(j), part]
            copies.append(remote(at, at, r2_send.at[c, j], r2_recv.at[c, j], (cpeer, rho)))
        return copies

    def second_in(c):
        part = pl.ds(c * GROUP, GROUP)
        copies = []
        for j in range(nz):
            at = lbuf.at[((mz + (nz - j)) % nz) * 2 + (1 - mx), part]
            copies.append(remote(at, at, l2_send.at[c, j], l2_recv.at[c, j], (lam, xpeer)))
        for j in range(ny):
            at = rbuf.at[((my + (ny - j)) % ny) * 2 + (1 - mc), part]
            copies.append(remote(at, at, r2_send.at[c, j], r2_recv.at[c, j], (cpeer, rho)))
        return copies

    def start_first(c):
        for copy in first_hop(c):
            copy.start()

    def forward(c):
        for copy in first_in(c):
            copy.wait_recv()
        for copy in second_hop(c):
            copy.start()

    for c in range(AHEAD):
        start_first(c)

    @pl.when(has_dn_r)
    def _():
        r_up.wait_recv()
        pl.when(has_up_l)(l_low[0].start)
        pl.when(has_dn_l)(l_low[1].start)

    @pl.when(has_up_r)
    def _():
        r_dn.wait_recv()
        pl.when(has_up_l)(l_high[0].start)
        pl.when(has_dn_l)(l_high[1].start)

    acc[...] = jnp.zeros_like(acc)
    own_l_copy.wait()
    own_r_copy.wait()
    forward(0)

    @pl.when(has_dn_l)
    def _():
        l_mid[0].wait_recv()
        pl.when(has_dn_r)(l_low[0].wait_recv)
        pl.when(has_up_r)(l_high[0].wait_recv)

    @pl.when(has_up_l)
    def _():
        l_mid[1].wait_recv()
        pl.when(has_dn_r)(l_low[1].wait_recv)
        pl.when(has_up_r)(l_high[1].wait_recv)

    def right_block(k, r):
        return rbuf[:, k, pl.ds(r * cb, cb), :].reshape(sb, sb)

    def left_block(k, l):
        if eb % 16 == 0:
            return lbuf[:, k, pl.ds(l * eb, eb), :].reshape(sb, sb)
        pieces = lbuf[:, k].astype(jnp.float32).reshape(nr, lc, eb, sb)
        return pieces[:, l].reshape(sb, sb).astype(jnp.bfloat16)

    def step(c, carry):
        @pl.when(c + AHEAD < chunks)
        def _():
            start_first(c + AHEAD)

        @pl.when(c + 1 < chunks)
        def _():
            forward(c + 1)

        for copy in second_in(c):
            copy.wait_recv()
        for g in range(GROUP):
            k = c * GROUP + g
            l_from = S - shift[k, 0]
            r_from = S - shift[k, 1]
            for r in range(rc):
                weights = right_block(k, r)
                for v in range(vectors):
                    source = xbuf[r_from + r, v, pl.ds(l_from, lc)].reshape(lc * sb, sb)
                    part = lax.dot_general(
                        source, weights, (((1,), (1,)), ((), ())),
                        preferred_element_type=jnp.float32,
                    ).astype(jnp.bfloat16)
                    pbuf[:, pl.ds(g * sb, sb), pl.ds((v * rc + r) * sb, sb)] = part.reshape(lc, sb, sb)
        for l in range(lc):
            left = jnp.concatenate(
                [left_block(c * GROUP + g, l) for g in range(GROUP)], axis=1
            )
            acc[l] += jnp.dot(left, pbuf[l], preferred_element_type=jnp.float32)
        return carry

    lax.fori_loop(0, chunks, step, 0)

    for l in range(lc):
        for r in range(rc):
            live = ((rows < lsize[l]) & (cols < rsize[r])).astype(jnp.float32)
            for v in range(vectors):
                block = acc[l, :, pl.ds((v * rc + r) * sb, sb)]
                out[v, l, :, pl.ds(r * sb, sb)] = (block * live).astype(out.dtype)

    def drain(c, carry):
        for copy in first_hop(c) + second_hop(c):
            copy.wait_send()
        return carry

    lax.fori_loop(0, chunks, drain, 0)
    pl.when(has_up_r)(r_up.wait_send)
    pl.when(has_dn_r)(r_dn.wait_send)
    for pair, there in ((l_mid, None), (l_low, has_dn_r), (l_high, has_up_r)):
        for copy, to in zip(pair, (has_up_l, has_dn_l)):
            pl.when(to if there is None else to & there)(copy.wait_send)


def local(nl, nr, two_site, left_env, right_env, left_size, right_size, channel_shift):
    vectors, lc, sb, columns = two_site.shape
    channels, rc = right_env.shape[:2]
    chunks = channels // GROUP
    nz, ny = nr // 2, nl // 2
    left_rows = left_env.reshape(channels, -1, sb)
    right_rows = right_env.reshape(channels, -1, sb)
    smem = pl.BlockSpec(memory_space=pltpu.SMEM)
    hbm = pl.BlockSpec(memory_space=pl.ANY)
    dma = pltpu.SemaphoreType.DMA
    return pl.pallas_call(
        functools.partial(kernel, nl, nr),
        out_shape=jax.ShapeDtypeStruct(two_site.shape, jnp.bfloat16),
        in_specs=[smem, smem, smem, hbm, hbm, hbm],
        out_specs=pl.BlockSpec(memory_space=pltpu.VMEM),
        scratch_shapes=[
            pltpu.VMEM((rc + 2 * SHIFT, vectors, lc + 2 * SHIFT, sb, sb), jnp.bfloat16),
            pltpu.VMEM((nr,) + left_rows.shape, jnp.bfloat16),
            pltpu.VMEM((nl,) + right_rows.shape, jnp.bfloat16),
            pltpu.VMEM((lc, GROUP * sb, vectors * columns), jnp.bfloat16),
            pltpu.VMEM((lc, sb, vectors * columns), jnp.float32),
            dma((rc,)), dma((2,)), dma((2,)), dma((2,)), dma((3, 2)), dma((3, 2)),
            dma((chunks, nz - 1)), dma((chunks, nz - 1)), dma((chunks, nz)), dma((chunks, nz)),
            dma((chunks, ny - 1)), dma((chunks, ny - 1)), dma((chunks, ny)), dma((chunks, ny)),
        ],
        compiler_params=pltpu.CompilerParams(
            collective_id=0, has_side_effects=True, vmem_limit_bytes=48 * 1024 * 1024
        ),
        cost_estimate=pl.CostEstimate(
            flops=4 * vectors * lc * sb * columns * sb * channels,
            bytes_accessed=4 * two_site.size + 2 * left_env.size + 2 * right_env.size,
            transcendentals=0,
        ),
    )(left_size, right_size, channel_shift, two_site, left_rows, right_rows)


def solution(mesh):
    placed = (
        P(None, "lsec", None, "rsec"),
        P(None, "lsec", "rsec", None),
        P(None, "rsec", "lsec", None),
        P("lsec"),
        P("rsec"),
        P(),
    )
    body = functools.partial(local, mesh.shape["lsec"], mesh.shape["rsec"])
    return jax.shard_map(
        body, mesh=mesh, in_specs=placed, out_specs=P(None, "lsec", None, "rsec"), check_vma=False
    )
```

time: 1400 us -> 97.5 us (0.07)
  blocking collectives: 1040 us -> 0 us
  matrix products: 128 us -> 0 us
  local copies, waits for them, and re-layouts: 103 us -> 6.58 us
  Pallas kernels: 0 us -> 90.6 us
  waiting for transfers between devices: 45 us -> 0 us
  loops' own time: 44.5 us -> 0 us
    all_gather x34 -> x0, blocking collectives: 1040 us -> none  [left_blocks(): return lax.all_gather(own_piece, 'rsec', axis=1, tiled=True)]
    dot_general x34 -> x0, matrix products: 128 us -> none  [one_channel(): jnp.einsum('jit,xjtum->xjium', left_sector_tensor, right_reduced, preferr...]
    pallas_call x0 -> x1, Pallas kernels: none -> 90.6 us  [local(): pl.pallas_call(functools.partial(kernel, nl, nr), out_shape=jax.ShapeDtyp...]
    dynamic_slice x102 -> x0, local copies, waits for them, and re-layouts: 90.2 us -> none  [the longest x34 44.9 us: one_channel(): lax.dynamic_slice(enlarged_operand, (jnp.int32(0), row_start, col_start),...]
    another operation x1 -> x0, loops' own time: 44.5 us -> none  [local(): total = lax.fori_loop(0, KCH, one_channel, start_total)]
    ppermute x4 -> x0, waiting for transfers between devices: 44.3 us -> none  [the longest x2 39.9 us: with_halo(): before = lax.ppermute(last, axis, up)]
  transfers between devices with their start and end apart: 5 -> 0, of which waited for: 3 -> 0; matrix products, arithmetic and copies ran while one was open for 1% -> 0% of each run, Pallas kernels for 0% -> 0%
where the time goes in v1:
time: 97.5 us; the launch traced here: 97.2 us
  Pallas kernels  90.6 us (93%)
  local copies, waits for them, and re-layouts  6.58 us (7%)
    pallas_call x1, Pallas kernels, local(): pl.pallas_call(functools.partial(kernel, nl, nr), out_shape=jax.ShapeDtyp...  90.6 us
    unnamed x12, local copies, waits for them, and re-layouts  6.58 us

profile of v1, /device:TPU:0, one launch (start us, length us, event | category | flops | bytes accessed | tf_op | source)
XLA Modules:
  0.0 97.2 jit_solution(7869669828655562184)
XLA Ops:
  0.0 0.8 copy.7.shift
  0.8 0.0 copy-start
  0.8 1.2 %copy-done = bf16[34,4,32,128]{3,2,1,0:T(8,128)(2,1)S(1)} copy-done((bf16[34,4,32,128]{3,2,1,0:T(8,128)(2,1)S(1)}, bf16[34,4,32,128]{3,2,1,0:T(8,128)(2,1)}, u32[]{:S(2)}) %copy-start) | copy-done | bytes 1114136
  2.0 0.0 copy-start.1
  2.0 1.2 %copy-done.1 = bf16[2,4,128,512]{3,2,1,0:T(8,128)(2,1)S(1)} copy-done((bf16[2,4,128,512]{3,2,1,0:T(8,128)(2,1)S(1)}, bf16[2,4,128,512]{3,2,1,0:T(8,128)(2,1)}, u32[]{:S(2)}) %copy-start.1) | copy-done | bytes 1048600
  3.2 0.0 copy-start.2
  3.2 1.1 %copy-done.2 = bf16[34,4,16,128]{3,2,1,0:T(8,128)(2,1)S(1)} copy-done((bf16[34,4,16,128]{3,2,1,0:T(8,128)(2,1)S(1)}, bf16[34,4,16,128]{3,2,1,0:T(8,128)(2,1)}, u32[]{:S(2)}) %copy-start.2) | copy-done | bytes 557080
  4.3 0.0 copy-start.3
  4.3 0.7 copy-done.3
  5.0 0.0 copy-start.4
  5.0 0.7 copy-done.4
  5.6 90.6 %shard_map.64 = bf16[2,4,128,512]{3,2,1,0:T(8,128)(2,1)S(1)} custom-call(s32[4]{0:T(128)S(1)} %copy-done.3, s32[4]{0:T(128)S(1)} %copy-done.4, s32[34,2]{1,0:T(8,128)S(1)} %copy.7.shift, bf16[2,4,128,512]{3,2,1,0:T(8,128)(2,1)S(1)} %copy-done.1, bf16[34,64,128]{2,1,0:T(8,128)(2,1)S(1)} %bitcast.3, bf16[34,128,128]{2,1,0:T(8,128)(2,1)S(1)} %bitcast.2), custom_call_target="tpu_custom_call" | custom-call | flops 9126805504 | bytes 3768320 | tf_op jit(solution)/shard_map/pallas_call | solution.py:307
  96.2 1.0 %copy.9 = bf16[2,4,128,512]{3,2,1,0:T(8,128)(2,1)} copy(bf16[2,4,128,512]{3,2,1,0:T(8,128)(2,1)S(1)} %shard_map.64) | data formatting | bytes 2097152
Async XLA Ops:
  0.8 1.2 %copy-start = (bf16[34,4,32,128]{3,2,1,0:T(8,128)(2,1)S(1)}, bf16[34,4,32,128]{3,2,1,0:T(8,128)(2,1)}, u32[]{:S(2)}) copy-start(bf16[34,4,32,128]{3,2,1,0:T(8,128)(2,1)} %param.8) | copy-start | bytes 3342340
  2.0 1.2 %copy-start.1 = (bf16[2,4,128,512]{3,2,1,0:T(8,128)(2,1)S(1)}, bf16[2,4,128,512]{3,2,1,0:T(8,128)(2,1)}, u32[]{:S(2)}) copy-start(bf16[2,4,128,512]{3,2,1,0:T(8,128)(2,1)} %x_hbm.1) | copy-start | bytes 3145732
  3.2 1.1 %copy-start.2 = (bf16[34,4,16,128]{3,2,1,0:T(8,128)(2,1)S(1)}, bf16[34,4,16,128]{3,2,1,0:T(8,128)(2,1)}, u32[]{:S(2)}) copy-start(bf16[34,4,16,128]{3,2,1,0:T(8,128)(2,1)} %param.7) | copy-start | bytes 1671172
  4.3 0.7 copy-start.3
  5.0 0.7 copy-start.4

commit v2 on v1

--- a/solution.py
+++ b/solution.py
@@ -9,7 +9,7 @@
 
 SHIFT = 2
 GROUP = 2
-AHEAD = 3
+EARLY, RELAY, SECOND, THIRD = 4, 10, 8, 4
 MESH = pl.DeviceIdType.MESH
 
 
@@ -17,7 +17,7 @@
     nl, nr, lsize, rsize, shift, x_hbm, l_hbm, r_hbm, out,
     xbuf, lbuf, rbuf, pbuf, acc,
     x_sem, own_sem, rh_send, rh_recv, lh_send, lh_recv,
-    l1_send, l1_recv, l2_send, l2_recv, r1_send, r1_recv, r2_send, r2_recv,
+    l1_send, l1_recv, l2_send, l2_recv, far_send, r1_send, r1_recv, r2_send, r2_recv,
 ):
     vectors, lc, sb, columns = x_hbm.shape
     rc = columns // sb
@@ -90,6 +90,166 @@
     pl.when(lam == 0)(lambda: zero_l(0))
     pl.when(lam == nl - 1)(lambda: zero_l(S + lc))
 
+    pl.semaphore_wait(barrier, len(near))
+
+    relayed = nz == 4
+    relays = (mz == 1) | (mz == 2)
+    relay_to = jnp.where(mz == 2, 3, 0) * 2 + mx
+    relay_sem = jnp.where(mz == 2, 3, 1)
+
+    def near_z(j):
+        if not relayed or j == 2:
+            return True
+        return (mz != nz - 1) if j == 1 else (mz != 0)
+
+    def when(condition, action):
+        if condition is True:
+            action()
+        else:
+            pl.when(condition)(action)
+
+    def by_z(c):
+        return c % 3 == 2
+
+    def part_of(c):
+        return pl.ds(c * GROUP, GROUP)
+
+    def l_first(c, j, slot=None):
+        part = part_of(c)
+        return remote(
+            l_hbm.at[part], lbuf.at[rho if slot is None else slot, part],
+            l1_send.at[c, j - 1], l1_recv.at[c, j - 1], (lam, zto(j)),
+        )
+
+    def l_own(c):
+        part = part_of(c)
+        return remote(
+            l_hbm.at[part], lbuf.at[rho, part],
+            l2_send.at[c, 0], l2_recv.at[c, 0], (lam, xpeer),
+        )
+
+    def l_relay(c):
+        at = lbuf.at[zslot(2), part_of(c)]
+        return remote(at, at, far_send.at[c, 0], l1_recv.at[c, relay_sem - 1], (lam, relay_to))
+
+    def l_second_x(c, j):
+        at = lbuf.at[zslot(j), part_of(c)]
+        return remote(at, at, l2_send.at[c, j], l2_recv.at[c, j], (lam, xpeer))
+
+    def l_second_z(c, j):
+        at = lbuf.at[xpeer, part_of(c)]
+        return remote(at, at, l2_send.at[c, j], l2_recv.at[c, j], (lam, zto(j)))
+
+    def l_third(c):
+        at = lbuf.at[((mz + (nz - 2)) % nz) * 2 + (1 - mx), part_of(c)]
+        return remote(at, at, far_send.at[c, 1], l2_recv.at[c, relay_sem], (lam, relay_to))
+
+    def l_in(c, j):
+        at = lbuf.at[((mz + (nz - j)) % nz) * 2 + (1 - mx), part_of(c)]
+        return remote(at, at, l2_send.at[c, j], l2_recv.at[c, j], (lam, xpeer))
+
+    def r_first(c, j, slot=None):
+        part = part_of(c)
+        return remote(
+            r_hbm.at[part], rbuf.at[lam if slot is None else slot, part],
+            r1_send.at[c, j - 1], r1_recv.at[c, j - 1], (yto(j), rho),
+        )
+
+    def r_own(c):
+        part = part_of(c)
+        return remote(
+            r_hbm.at[part], rbuf.at[lam, part],
+            r2_send.at[c, 0], r2_recv.at[c, 0], (cpeer, rho),
+        )
+
+    def r_second(c, j):
+        at = rbuf.at[yslot(j), part_of(c)]
+        return remote(at, at, r2_send.at[c, j], r2_recv.at[c, j], (cpeer, rho))
+
+    def r_in(c, j):
+        at = rbuf.at[((my + (ny - j)) % ny) * 2 + (1 - mc), part_of(c)]
+        return remote(at, at, r2_send.at[c, j], r2_recv.at[c, j], (cpeer, rho))
+
+    def start_first(c):
+        for j in range(1, nz):
+            when(near_z(j), l_first(c, j).start)
+        l_own(c).start()
+        for j in range(1, ny):
+            r_first(c, j).start()
+        r_own(c).start()
+
+    def relay(c):
+        if relayed:
+            l_first(c, 2, zslot(2)).wait_recv()
+            pl.when(relays)(l_relay(c).start)
+
+    def second(c):
+        for j in range(1, ny):
+            r_first(c, j, yslot(j)).wait_recv()
+            r_second(c, j).start()
+        l_in(c, 0).wait_recv()
+
+        @pl.when(by_z(c))
+        def _():
+            for j in range(1, nz):
+                when(near_z(j), l_second_z(c, j).start)
+
+        for j in range(1, nz):
+            if not (relayed and j == 2):
+                l_first(c, j, zslot(j)).wait_recv()
+
+        @pl.when(jnp.logical_not(by_z(c)))
+        def _():
+            for j in range(1, nz):
+                l_second_x(c, j).start()
+
+    def third(c):
+        if relayed:
+            @pl.when(by_z(c))
+            def _():
+                l_in(c, 2).wait_recv()
+                pl.when(relays)(l_third(c).start)
+
+    def arrive(c):
+        for j in range(1, nz):
+            if relayed and j == 2:
+                pl.when(jnp.logical_not(by_z(c)))(l_in(c, j).wait_recv)
+            else:
+                l_in(c, j).wait_recv()
+        for j in range(ny):
+            r_in(c, j).wait_recv()
+
+    def sent(c):
+        for j in range(1, nz):
+            when(near_z(j), l_first(c, j).wait_send)
+        l_own(c).wait_send()
+        for j in range(1, ny):
+            r_first(c, j).wait_send()
+            r_second(c, j).wait_send()
+        r_own(c).wait_send()
+        if relayed:
+            pl.when(relays)(l_relay(c).wait_send)
+            pl.when(relays & by_z(c))(l_third(c).wait_send)
+
+        @pl.when(by_z(c))
+        def _():
+            for j in range(1, nz):
+                when(near_z(j), l_second_z(c, j).wait_send)
+
+        @pl.when(jnp.logical_not(by_z(c)))
+        def _():
+            for j in range(1, nz):
+                l_second_x(c, j).wait_send()
+
+    def each(begin, end, action):
+        def body(c, carry):
+            action(c)
+            return carry
+
+        lax.fori_loop(begin, end, body, 0)
+
+    each(0, EARLY, start_first)
+
     rows = lax.broadcasted_iota(jnp.int32, (sb, sb), 0)
     cols = lax.broadcasted_iota(jnp.int32, (sb, sb), 1)
     for r in range(rc):
@@ -100,8 +260,6 @@
                 block = xbuf[S + r, v, S + l].astype(jnp.float32)
                 xbuf[S + r, v, S + l] = (block * live).astype(xbuf.dtype)
 
-    pl.semaphore_wait(barrier, len(near))
-
     r_up = remote(
         xbuf.at[pl.ds(rc, S), :, own_l], xbuf.at[pl.ds(0, S), :, own_l],
         rh_send.at[0], rh_recv.at[0], (lam, rho + 1),
@@ -130,78 +288,8 @@
     pl.when(has_up_l)(l_mid[0].start)
     pl.when(has_dn_l)(l_mid[1].start)
 
-    def first_hop(c):
-        part = pl.ds(c * GROUP, GROUP)
-        copies = []
-        for j in range(1, nz):
-            copies.append(remote(
-                l_hbm.at[part], lbuf.at[rho, part],
-                l1_send.at[c, j - 1], l1_recv.at[c, j - 1], (lam, zto(j)),
-            ))
-        for j in range(1, ny):
-            copies.append(remote(
-                r_hbm.at[part], rbuf.at[lam, part],
-                r1_send.at[c, j - 1], r1_recv.at[c, j - 1], (yto(j), rho),
-            ))
-        copies.append(remote(
-            l_hbm.at[part], lbuf.at[rho, part],
-            l2_send.at[c, 0], l2_recv.at[c, 0], (lam, xpeer),
-        ))
-        copies.append(remote(
-            r_hbm.at[part], rbuf.at[lam, part],
-            r2_send.at[c, 0], r2_recv.at[c, 0], (cpeer, rho),
-        ))
-        return copies
-
-    def first_in(c):
-        part = pl.ds(c * GROUP, GROUP)
-        copies = []
-        for j in range(1, nz):
-            copies.append(remote(
-                l_hbm.at[part], lbuf.at[zslot(j), part],
-                l1_send.at[c, j - 1], l1_recv.at[c, j - 1], (lam, zto(j)),
-            ))
-        for j in range(1, ny):
-            copies.append(remote(
-                r_hbm.at[part], rbuf.at[yslot(j), part],
-                r1_send.at[c, j - 1], r1_recv.at[c, j - 1], (yto(j), rho),
-            ))
-        return copies
-
-    def second_hop(c):
-        part = pl.ds(c * GROUP, GROUP)
-        copies = []
-        for j in range(1, nz):
-            at = lbuf.at[zslot(j), part]
-            copies.append(remote(at, at, l2_send.at[c, j], l2_recv.at[c, j], (lam, xpeer)))
-        for j in range(1, ny):
-            at = rbuf.at[yslot(j), part]
-            copies.append(remote(at, at, r2_send.at[c, j], r2_recv.at[c, j], (cpeer, rho)))
-        return copies
-
-    def second_in(c):
-        part = pl.ds(c * GROUP, GROUP)
-        copies = []
-        for j in range(nz):
-            at = lbuf.at[((mz + (nz - j)) % nz) * 2 + (1 - mx), part]
-            copies.append(remote(at, at, l2_send.at[c, j], l2_recv.at[c, j], (lam, xpeer)))
-        for j in range(ny):
-            at = rbuf.at[((my + (ny - j)) % ny) * 2 + (1 - mc), part]
-            copies.append(remote(at, at, r2_send.at[c, j], r2_recv.at[c, j], (cpeer, rho)))
-        return copies
-
-    def start_first(c):
-        for copy in first_hop(c):
-            copy.start()
-
-    def forward(c):
-        for copy in first_in(c):
-            copy.wait_recv()
-        for copy in second_hop(c):
-            copy.start()
-
-    for c in range(AHEAD):
-        start_first(c)
+    each(EARLY, chunks, start_first)
+    each(0, EARLY, relay)
 
     @pl.when(has_dn_r)
     def _():
@@ -218,7 +306,10 @@
     acc[...] = jnp.zeros_like(acc)
     own_l_copy.wait()
     own_r_copy.wait()
-    forward(0)
+
+    each(EARLY, RELAY, relay)
+    each(0, SECOND, second)
+    each(0, THIRD, third)
 
     @pl.when(has_dn_l)
     def _():
@@ -242,16 +333,10 @@
         return pieces[:, l].reshape(sb, sb).astype(jnp.bfloat16)
 
     def step(c, carry):
-        @pl.when(c + AHEAD < chunks)
-        def _():
-            start_first(c + AHEAD)
-
-        @pl.when(c + 1 < chunks)
-        def _():
-            forward(c + 1)
-
-        for copy in second_in(c):
-            copy.wait_recv()
+        pl.when(c + RELAY < chunks)(lambda: relay(c + RELAY))
+        pl.when(c + SECOND < chunks)(lambda: second(c + SECOND))
+        pl.when(c + THIRD < chunks)(lambda: third(c + THIRD))
+        arrive(c)
         for g in range(GROUP):
             k = c * GROUP + g
             l_from = S - shift[k, 0]
@@ -281,12 +366,7 @@
                 block = acc[l, :, pl.ds((v * rc + r) * sb, sb)]
                 out[v, l, :, pl.ds(r * sb, sb)] = (block * live).astype(out.dtype)
 
-    def drain(c, carry):
-        for copy in first_hop(c) + second_hop(c):
-            copy.wait_send()
-        return carry
-
-    lax.fori_loop(0, chunks, drain, 0)
+    each(0, chunks, sent)
     pl.when(has_up_r)(r_up.wait_send)
     pl.when(has_dn_r)(r_dn.wait_send)
     for pair, there in ((l_mid, None), (l_low, has_dn_r), (l_high, has_up_r)):
@@ -317,10 +397,11 @@
             pltpu.VMEM((lc, sb, vectors * columns), jnp.float32),
             dma((rc,)), dma((2,)), dma((2,)), dma((2,)), dma((3, 2)), dma((3, 2)),
             dma((chunks, nz - 1)), dma((chunks, nz - 1)), dma((chunks, nz)), dma((chunks, nz)),
+            dma((chunks, 2)),
             dma((chunks, ny - 1)), dma((chunks, ny - 1)), dma((chunks, ny)), dma((chunks, ny)),
         ],
         compiler_params=pltpu.CompilerParams(
-            collective_id=0, has_side_effects=True, vmem_limit_bytes=48 * 1024 * 1024
+            collective_id=0, has_side_effects=True, vmem_limit_bytes=60 * 1024 * 1024
         ),
         cost_estimate=pl.CostEstimate(
             flops=4 * vectors * lc * sb * columns * sb * channels,

time: 97.5 us -> 88.5 us (0.908)
  Pallas kernels: 90.6 us -> 84.6 us
  local copies, waits for them, and re-layouts: 6.58 us -> 3.63 us
    pallas_call x1, Pallas kernels: 90.6 us -> 84.6 us  [local(): pl.pallas_call(functools.partial(kernel, nl, nr), out_shape=jax.ShapeDtyp...]
    unnamed x12 -> x2, local copies, waits for them, and re-layouts: 6.58 us -> 3.63 us
where the time goes in v2:
time: 88.5 us; the launch traced here: 88.2 us
  Pallas kernels  84.6 us (96%)
  local copies, waits for them, and re-layouts  3.63 us (4%)
    pallas_call x1, Pallas kernels, local(): pl.pallas_call(functools.partial(kernel, nl, nr), out_shape=jax.ShapeDtyp...  84.6 us
    unnamed x2, local copies, waits for them, and re-layouts  3.63 us

profile of v2, /device:TPU:0, one launch (start us, length us, event | category | flops | bytes accessed | tf_op | source)
XLA Modules:
  0.0 88.2 jit_solution(2722814887646375420)
XLA Ops:
  0.0 1.4 %copy.7.shift = s32[34,2]{1,0:T(8,128)} copy(s32[34,2]{0,1:T(2,128)} %param.11) | data formatting | bytes 544 | tf_op args[5]
  1.4 84.6 %shard_map.64 = bf16[2,4,128,512]{3,2,1,0:T(8,128)(2,1)} custom-call(s32[4]{0:T(128)} %lsize.1, s32[4]{0:T(128)} %rsize.1, s32[34,2]{1,0:T(8,128)} %copy.7.shift, bf16[2,4,128,512]{3,2,1,0:T(8,128)(2,1)} %x_hbm.1, bf16[34,64,128]{2,1,0:T(8,128)(2,1)} %bitcast.3, bf16[34,128,128]{2,1,0:T(8,128)(2,1)} %bitcast.2), custom_call_target="tpu_custom_call" | custom-call | flops 9126805504 | bytes 3768320 | tf_op jit(solution)/shard_map/pallas_call | solution.py:387
  85.9 2.3 %copy.9 = bf16[2,4,128,512]{3,2,1,0:T(8,128)(2,1)} copy(bf16[2,4,128,512]{3,2,1,0:T(8,128)(2,1)} %shard_map.64) | data formatting | bytes 2097152

commit v3 on v1

--- a/solution.py
+++ b/solution.py
@@ -9,7 +9,7 @@
 
 SHIFT = 2
 GROUP = 2
-AHEAD = 3
+AHEAD = 8
 MESH = pl.DeviceIdType.MESH
 
 
@@ -200,8 +200,11 @@
         for copy in second_hop(c):
             copy.start()
 
-    for c in range(AHEAD):
+    def start_chunk(c, carry):
         start_first(c)
+        return carry
+
+    lax.fori_loop(0, chunks, start_chunk, 0)
 
     @pl.when(has_dn_r)
     def _():
@@ -218,7 +221,12 @@
     acc[...] = jnp.zeros_like(acc)
     own_l_copy.wait()
     own_r_copy.wait()
-    forward(0)
+
+    def forward_chunk(c, carry):
+        forward(c)
+        return carry
+
+    lax.fori_loop(0, AHEAD, forward_chunk, 0)
 
     @pl.when(has_dn_l)
     def _():
@@ -244,11 +252,7 @@
     def step(c, carry):
         @pl.when(c + AHEAD < chunks)
         def _():
-            start_first(c + AHEAD)
-
-        @pl.when(c + 1 < chunks)
-        def _():
-            forward(c + 1)
+            forward(c + AHEAD)
 
         for copy in second_in(c):
             copy.wait_recv()
@@ -320,7 +324,7 @@
             dma((chunks, ny - 1)), dma((chunks, ny - 1)), dma((chunks, ny)), dma((chunks, ny)),
         ],
         compiler_params=pltpu.CompilerParams(
-            collective_id=0, has_side_effects=True, vmem_limit_bytes=48 * 1024 * 1024
+            collective_id=0, has_side_effects=True, vmem_limit_bytes=60 * 1024 * 1024
         ),
         cost_estimate=pl.CostEstimate(
             flops=4 * vectors * lc * sb * columns * sb * channels,

time: 97.5 us -> 85.8 us (0.88)
  Pallas kernels: 90.6 us -> 81.3 us
  local copies, waits for them, and re-layouts: 6.58 us -> 3.63 us
    pallas_call x1, Pallas kernels: 90.6 us -> 81.3 us  [local(): pl.pallas_call(functools.partial(kernel, nl, nr), out_shape=jax.ShapeDtyp...]
    unnamed x12 -> x2, local copies, waits for them, and re-layouts: 6.58 us -> 3.63 us
where the time goes in v3:
time: 85.8 us; the launch traced here: 84.9 us
  Pallas kernels  81.3 us (95%)
  local copies, waits for them, and re-layouts  3.63 us (4%)
    pallas_call x1, Pallas kernels, local(): pl.pallas_call(functools.partial(kernel, nl, nr), out_shape=jax.ShapeDtyp...  81.3 us
    unnamed x2, local copies, waits for them, and re-layouts  3.63 us

profile of v3, /device:TPU:0, one launch (start us, length us, event | category | flops | bytes accessed | tf_op | source)
XLA Modules:
  0.0 84.9 jit_solution(13627379416997269086)
XLA Ops:
  0.0 1.4 %copy.7.shift = s32[34,2]{1,0:T(8,128)} copy(s32[34,2]{0,1:T(2,128)} %param.11) | data formatting | bytes 544 | tf_op args[5]
  1.4 81.3 %shard_map.64 = bf16[2,4,128,512]{3,2,1,0:T(8,128)(2,1)} custom-call(s32[4]{0:T(128)} %lsize.1, s32[4]{0:T(128)} %rsize.1, s32[34,2]{1,0:T(8,128)} %copy.7.shift, bf16[2,4,128,512]{3,2,1,0:T(8,128)(2,1)} %x_hbm.1, bf16[34,64,128]{2,1,0:T(8,128)(2,1)} %bitcast.3, bf16[34,128,128]{2,1,0:T(8,128)(2,1)} %bitcast.2), custom_call_target="tpu_custom_call" | custom-call | flops 9126805504 | bytes 3768320 | tf_op jit(solution)/shard_map/pallas_call | solution.py:311
  82.7 2.3 %copy.9 = bf16[2,4,128,512]{3,2,1,0:T(8,128)(2,1)} copy(bf16[2,4,128,512]{3,2,1,0:T(8,128)(2,1)} %shard_map.64) | data formatting | bytes 2097152
